TPU v7x, 32 devices: a whole 2x2x4 slice. The times are simulated.
32 devices in a mesh: parts: 2 (over y), rows: 16 (over z, x, core).
Axes of the slice: x: 2, y: 2, z: 4, core: 2. Of those that a mesh axis runs over, the one named last changes fastest.
Arguments:
- factor_panels: float32 [16384, 1536], P(('parts', 'rows')), parts along dimension 0, as said below
- targets: float32 [16384, 256], P(('parts', 'rows')), parts along dimension 0, may hold values from -6 to 6
- later_solutions: float32 [16384, 256], P(('parts', 'rows')), parts along dimension 0, as said below
Outputs:
- solved_rows: float32 [16384, 256], P(('parts', 'rows')), parts along dimension 0
There are 2 independent parts, one for each index of `parts`. A program takes and returns all parts, laid end to end along the dimension named above; each array names one. Nothing has to cross between parts.
Inputs may be any that keep to these rules, and one draw needn't show every extreme that they name: `factor_panels`: in rows of block d < 3, column blocks above d are zero and column block d holds a lower-triangular inverse diagonal block. `later_solutions`: the first 1536 rows are zero.
All inputs are finite; a program needn't handle non-finite values.
Results may differ from a plain program's by a relative error of at most 0.0001.
Values sent between devices are 32-bit elements; how exact they have to be, the bound alone decides.
A program may use at most 64 MiB of HBM per device.

v0:
```python
import jax
import jax.numpy as jnp
from jax import lax
from jax.sharding import PartitionSpec as P

exact_mode = lax.Precision.HIGHEST


def broadcast(shard, axis, root):
    mine = lax.axis_index(axis) == root
    return lax.psum(jnp.where(mine, shard, jnp.zeros_like(shard)), axis)


def product(left, right):
    return jnp.dot(left, right, precision=exact_mode, preferred_element_type=jnp.float32)


def transposed(left, right):
    return lax.dot_general(
        left,
        right,
        (((0,), (0,)), ((), ())),
        precision=exact_mode,
        preferred_element_type=jnp.float32,
    )


def local(factor_panels, targets, later_solutions):
    device = lax.axis_index("rows")
    block_rows = factor_panels.shape[0]
    panels = factor_panels.shape[1] // block_rows

    def panel_cols(panel):
        return factor_panels[:, panel * block_rows : (panel + 1) * block_rows]

    solved = []
    residual = targets
    for panel in range(panels):
        candidate = product(panel_cols(panel), residual)
        forward_part = broadcast(candidate, "rows", panel)
        solved.append(forward_part)
        residual = jnp.where(
            device > panel, residual - product(panel_cols(panel), forward_part), residual
        )
    answer = later_solutions
    for panel in reversed(range(panels)):
        partial_terms = jnp.where(device > panel, transposed(panel_cols(panel), answer), 0.0)
        fan_sum = lax.psum(partial_terms, "rows")
        candidate = transposed(panel_cols(panel), solved[panel] - fan_sum)
        answer = jnp.where(device == panel, candidate, answer)
    return jnp.where(device < panels, answer, residual)


def solution(mesh):
    in_specs = (P(("parts", "rows"), None), P(("parts", "rows"), None), P(("parts", "rows"), None))
    out_specs = P(("parts", "rows"), None)
    return jax.shard_map(local, mesh=mesh, in_specs=in_specs, out_specs=out_specs, check_vma=False)
```

profile of v0, /device:TPU:0, one launch (start us, length us, event | category | flops | bytes accessed | tf_op | source)
XLA Modules:
  0.0 503.2 jit_solution(16484655578196028900)
XLA Ops:
  6.5 0.0 copy-start
  6.5 0.0 all-reduce.7.cloned.1.call-start
  6.5 3.3 convolution_select_fusion.5
  9.8 0.0 all-reduce.7.cloned.1.call-update
  9.9 0.0 all-reduce.9.cloned.1.call-start
  9.9 93.7 %all-reduce.7.cloned.1.call-done = f32[512,256]{1,0:T(8,128)} async-done(((f32[512,256]{1,0:T(8,128)}), f32[512,256]{1,0:T(8,128)}) %all-reduce.7.cloned.1.call-update) | async-done | bytes 524304 | tf_op jit(solution)/shard_map/psum | solution.py:11
  103.6 2.5 fusion.13
  106.1 0.0 copy-start.5
  106.2 0.8 copy-done.5
  106.9 0.0 copy-done
  106.9 1.8 fusion.11
  108.7 0.0 all-reduce.9.cloned.1.call-update
  108.8 0.0 all-reduce.15.cloned.1.call-start
  108.8 3.7 convolution_select_fusion.2
  112.5 87.0 %all-reduce.9.cloned.1.call-done = f32[512,256]{1,0:T(8,128)} async-done(((f32[512,256]{1,0:T(8,128)}), f32[512,256]{1,0:T(8,128)}) %all-reduce.9.cloned.1.call-update) | async-done | bytes 524304 | tf_op jit(solution)/shard_map/psum | solution.py:11
  199.5 2.2 fusion.10
  201.7 0.0 copy-start.1
  201.7 0.8 copy-done.1
  202.5 1.8 fusion.8
  204.3 0.0 all-reduce.15.cloned.1.call-update
  204.3 0.0 all-reduce.11.cloned.1.call-start
  204.4 93.8 %all-reduce.15.cloned.1.call-done = (f32[512,256]{1,0:T(8,128)}, f32[512,256]{1,0:T(8,128)}) async-done(((f32[512,256]{1,0:T(8,128)}, f32[512,256]{1,0:T(8,128)}), (f32[512,256]{1,0:T(8,128)}, f32[512,256]{1,0:T(8,128)})) %all-reduce.15.cloned.1.call-update) | async-done | bytes 1048592 | tf_op jit(solution)/shard_map/psum | solution.py:11
  298.2 3.2 fusion.7
  301.4 0.0 copy-start.4
  301.4 0.8 copy-done.4
  302.2 2.6 fusion.6
  304.8 0.0 all-reduce.11.cloned.1.call-update
  304.8 0.2 all-reduce.13.cloned.1.call-start
  305.0 89.3 %all-reduce.11.cloned.1.call-done = f32[512,256]{1,0:T(8,128)} async-done(((f32[512,256]{1,0:T(8,128)}), f32[512,256]{1,0:T(8,128)}) %all-reduce.11.cloned.1.call-update) | async-done | bytes 524304 | tf_op jit(solution)/shard_map/psum | solution.py:48
  394.4 3.2 fusion.5
  397.5 0.0 copy-start.3
  397.6 0.8 copy-done.3
  398.3 2.6 fusion.4
  401.0 0.0 all-reduce.13.cloned.1.call-update
  401.0 90.7 %all-reduce.13.cloned.1.call-done = f32[512,256]{1,0:T(8,128)} async-done(((f32[512,256]{1,0:T(8,128)}), f32[512,256]{1,0:T(8,128)}) %all-reduce.13.cloned.1.call-update) | async-done | bytes 524304 | tf_op jit(solution)/shard_map/psum | solution.py:48
  491.7 0.0 copy-start.2
  491.7 0.0 copy-start.6
  491.7 3.1 fusion.3
  494.8 0.0 copy-done.2
  494.8 0.0 copy-done.6
  494.8 1.8 fusion.2
Async XLA Ops:
  6.5 100.4 %copy-start = (f32[512,1536]{1,0:T(8,128)S(1)}, f32[512,1536]{1,0:T(8,128)}, u32[]{:S(2)}) copy-start(f32[512,1536]{1,0:T(8,128)} %param.3) | copy-start | bytes 9437188
  6.5 97.1 %all-reduce.7.cloned.1.call-start = ((), (), s32[]{:S(2)}) async-start(), calls=%async_computation | async-start | bytes 1048576 | tf_op jit(solution)/shard_map/psum | solution.py:11
  9.9 189.6 %all-reduce.9.cloned.1.call-start = ((), (), s32[]{:S(2)}) async-start(), calls=%async_computation.1 | async-start | bytes 1048576 | tf_op jit(solution)/shard_map/psum | solution.py:11
  106.1 0.8 copy-start.5
  108.8 189.4 %all-reduce.15.cloned.1.call-start = ((), (), s32[]{:S(2)}) async-start(), calls=%async_computation.4 | async-start | bytes 2097152 | tf_op jit(solution)/shard_map/psum | solution.py:11
  201.7 0.8 copy-start.1
  204.3 190.1 %all-reduce.11.cloned.1.call-start = ((), (), s32[]{:S(2)}) async-start(), calls=%async_computation.2 | async-start | bytes 1048576 | tf_op jit(solution)/shard_map/psum | solution.py:48
  301.4 0.8 copy-start.4
  304.8 186.9 %all-reduce.13.cloned.1.call-start = ((), (), s32[]{:S(2)}) async-start(), calls=%async_computation.3 | async-start | bytes 1048576 | tf_op jit(solution)/shard_map/psum | solution.py:48
  397.5 0.8 copy-start.3
  491.7 3.1 copy-start.2
  491.7 3.1 copy-start.6
Sparse Core Ops, SparseCore 0:
  10.8 92.7 all-reduce.6
  108.9 90.5 all-reduce.8
  204.4 93.7 all-reduce.14
  304.9 89.3 all-reduce.10
  401.1 90.5 all-reduce.12
where the time goes:
time: 504 us; the launch traced here: 503 us
  waiting for transfers between devices  455 us (90%)
  matrix products  31.8 us (6%)
  between operations  13.3 us (3%)
    psum x3, waiting for transfers between devices, broadcast(): return lax.psum(jnp.where(mine, shard, jnp.zeros_like(shard)), axis)  275 us
    psum x2, waiting for transfers between devices, local(): fan_sum = lax.psum(partial_terms, 'rows')  180 us
    dot_general x6, matrix products, transposed(): lax.dot_general(left, right, (((0,), (0,)), ((), ())), precision=exact_mo...  18.3 us
    dot_general x6, matrix products, product(): jnp.dot(left, right, precision=exact_mode, preferred_element_type=jnp.flo...  13.5 us
  transfers between devices with their start and end apart: 5, of which 5 were waited for; matrix products, arithmetic and copies ran while one was open for 1% of the time, Pallas kernels for 0%

commit v1 on v0

v1 whole, which is shorter than its diff:
```python
import functools

import jax
import jax.numpy as jnp
from jax import lax
from jax.experimental import pallas as pl
from jax.experimental.pallas import tpu as pltpu
from jax.sharding import PartitionSpec as P

MESH = pl.DeviceIdType.MESH
PLANE = 4
SUBS = 2
GROUPS = 2


def split(value):
    high = value.astype(jnp.bfloat16)
    return high, (value - high.astype(jnp.float32)).astype(jnp.bfloat16)


def triple(left, right, contract):
    def one(a, b):
        return lax.dot_general(
            a, b, (((1,), (contract,)), ((), ())), preferred_element_type=jnp.float32
        )

    return one(left[0], right[0]) + (one(left[0], right[1]) + one(left[1], right[0]))


def kernel(
    devices, panels,
    p_hbm, t_hbm, later_hbm, out_ref,
    p_ref, t_ref, later_ref, p_high, p_low,
    y_ref, term, from_core, from_x, from_z, part_x, part_z, fan, send_w, got_w,
    in_sem, send_sem, y_sem, core_sem, x_sem, z_sem, fan_sem, w_sem,
):
    block, rhs = t_ref.shape
    levels = devices // PLANE
    piece = rhs // PLANE // SUBS
    group = rhs // GROUPS
    me = lax.axis_index("rows")
    level, q = me // PLANE, me % PLANE
    x, core = q // 2, q % 2
    mine = core * 2 + x
    facing = core * 2 + 1 - x
    sibling = me + 1 - 2 * core
    across = me + 2 - 4 * x
    up, down = me - PLANE, me + PLANE

    loads = {"t": pltpu.make_async_copy(t_hbm, t_ref, in_sem.at[0])}
    loads["later"] = pltpu.make_async_copy(later_hbm, later_ref, in_sem.at[1])
    for k in range(panels):
        loads[k] = pltpu.make_async_copy(
            p_hbm.at[:, k * block : (k + 1) * block], p_ref.at[k], in_sem.at[2 + k]
        )
    for name in ["t", 0, "later"] + list(range(panels - 1, 0, -1)):
        loads[name].start()

    barrier = pltpu.get_barrier_semaphore()
    for step in range(1, PLANE):
        other = level * PLANE + (q + step) % PLANE
        pl.semaphore_signal(barrier, inc=1, device_id={"rows": other}, device_id_type=MESH)

    @pl.when(level > 0)
    def _():
        pl.semaphore_signal(barrier, inc=1, device_id={"rows": up}, device_id_type=MESH)

    @pl.when(level < levels - 1)
    def _():
        pl.semaphore_signal(barrier, inc=1, device_id={"rows": down}, device_id_type=MESH)

    inner = jnp.logical_and(level > 0, level < levels - 1)

    @pl.when(inner)
    def _():
        pl.semaphore_wait(barrier, PLANE + 1)

    @pl.when(jnp.logical_not(inner))
    def _():
        pl.semaphore_wait(barrier, PLANE)

    class Sends:
        def __init__(self):
            self.held = []

        def __call__(self, src, dst, recv, device, when=None):
            copy = pltpu.make_async_remote_copy(
                src_ref=src, dst_ref=dst, send_sem=send_sem.at[len(self.held)], recv_sem=recv,
                device_id={"rows": device}, device_id_type=MESH,
            )
            self.held.append((copy, when))
            if when is None:
                copy.start()
            else:
                pl.when(when)(copy.start)

        def finish(self):
            for copy, when in self.held:
                if when is None:
                    copy.wait_send()
                else:
                    pl.when(when)(copy.wait_send)

    def arrive(ref, sem):
        pltpu.make_async_remote_copy(
            src_ref=ref, dst_ref=ref, send_sem=send_sem.at[0], recv_sem=sem,
            device_id={"rows": sibling}, device_id_type=MESH,
        ).wait_recv()

    def send_y(send, k, at, h, device, when=None):
        send(y_ref.at[k, at, h], y_ref.at[k, at, h], y_sem.at[k, at, h], device, when)

    def wait_y(k, at, h):
        arrive(y_ref.at[k, at, h], y_sem.at[k, at, h])

    def y_value(k, g=None):
        value = y_ref[k].reshape(rhs, block)
        return value if g is None else value[g * group : (g + 1) * group]

    def y_group(k, g):
        per = PLANE // GROUPS
        return y_ref[k, g * per : (g + 1) * per].reshape(group, block)

    def fan_group(g):
        per = PLANE // GROUPS
        return fan[g * per : (g + 1) * per].reshape(group, block)

    def store_y(k, g, value):
        per = PLANE // GROUPS
        y_ref[k, g * per : (g + 1) * per] = value.reshape(per, SUBS, piece, block)

    def load_panel(k):
        loads[k].wait()
        high, low = split(p_ref[k])
        p_high[k] = high
        p_low[k] = low

    def panel(k):
        return p_high[k], p_low[k]

    def in_group(g):
        per = PLANE // GROUPS
        return range(g * per, (g + 1) * per)

    def rows_of(g):
        return pl.ds(g * group, group)

    def relay(send, k, owner_is_me, own_term):
        for h in range(SUBS):
            if own_term:
                value = term[k, mine, h]
            else:
                arrive(from_x.at[k, h], x_sem.at[k, h])
                value = from_x[k, h]
            arrive(from_z.at[k, h], z_sem.at[k, h])
            value = value + from_z[k, h]
            if owner_is_me:
                fan[mine, h] = value
            else:
                part_z[k, h] = value
                send(part_z.at[k, h], fan.at[mine, h], fan_sem.at[mine, h], k)

    def fan_wait(owner, g):
        own = (owner % 2) * 2 + owner // 2
        for at in in_group(g):
            if at != own:
                for h in range(SUBS):
                    arrive(fan.at[at, h], fan_sem.at[at, h])

    def send_w_group(send, slot, to_slot, g, device):
        send(send_w.at[slot, rows_of(g)], got_w.at[to_slot, rows_of(g)], w_sem.at[to_slot, g], device)

    def wait_w(slot, g):
        arrive(got_w.at[slot, rows_of(g)], w_sem.at[slot, g])

    def drain(names):
        for name in names:
            loads[name].wait()

    @pl.when(me == 0)
    def _():
        send = Sends()
        loads["t"].wait()
        load_panel(0)
        target = t_ref[...].T
        for g in range(GROUPS):
            store_y(0, g, triple(split(target[g * group : (g + 1) * group]), panel(0), 1))
            for at in in_group(g):
                for h in range(SUBS):
                    send_y(send, 0, at, h, 1)
                    send_y(send, 0, at, h, 2)
                    if at == 0:
                        send_y(send, 0, at, h, PLANE)
        drain(["later", 1, 2])
        for h in range(SUBS):
            wait_y(1, 0, h)
            send_y(send, 1, 0, h, PLANE)
        relay(send, 2, False, False)
        relay(send, 1, False, False)
        for h in range(SUBS):
            wait_y(2, 0, h)
            send_y(send, 2, 0, h, PLANE)
        relay(send, 0, True, False)
        for g in range(GROUPS):
            fan_wait(0, g)
            wait_w(0, g)
            right = y_group(0, g) - fan_group(g) - got_w[0, rows_of(g)]
            wait_w(1, g)
            answer = triple(split(right - got_w[1, rows_of(g)]), panel(0), 0)
            out_ref[:, g * group : (g + 1) * group] = answer.T
        send.finish()

    @pl.when(me == 1)
    def _():
        send = Sends()
        loads["t"].wait()
        target = t_ref[...].T
        load_panel(0)
        load_panel(1)
        for g in range(GROUPS):
            for at in in_group(g):
                for h in range(SUBS):
                    wait_y(0, at, h)
                    if at == 2:
                        send_y(send, 0, at, h, 1 + PLANE)
            right = target[g * group : (g + 1) * group] - triple(split(y_group(0, g)), panel(0), 1)
            store_y(1, g, triple(split(right), panel(1), 1))
            for at in in_group(g):
                for h in range(SUBS):
                    send_y(send, 1, at, h, 2)
                    if at == 2:
                        send_y(send, 1, at, h, 1 + PLANE)
                    if at == 0:
                        send_y(send, 1, at, h, 0)
        drain(["later", 2])
        relay(send, 2, False, False)
        relay(send, 1, True, False)
        for h in range(SUBS):
            wait_y(2, 2, h)
            send_y(send, 2, 2, h, 1 + PLANE)
        relay(send, 0, False, False)
        for g in range(GROUPS):
            fan_wait(1, g)
            right = y_group(1, g) - fan_group(g)
            wait_w(0, g)
            answer = triple(split(right - got_w[0, rows_of(g)]), panel(1), 0)
            send_w[0, rows_of(g)] = triple(split(answer), panel(0), 0)
            send_w_group(send, 0, 1, g, 0)
            out_ref[:, g * group : (g + 1) * group] = answer.T
        send.finish()

    @pl.when(me == 2)
    def _():
        send = Sends()
        loads["t"].wait()
        target = t_ref[...].T
        for k in range(panels):
            load_panel(k)
        for g in range(GROUPS):
            right = target[g * group : (g + 1) * group]
            for k in range(2):
                for at in in_group(g):
                    for h in range(SUBS):
                        wait_y(k, at, h)
                        send_y(send, k, at, h, 3)
                        if at == 1:
                            send_y(send, k, at, h, 2 + PLANE)
                right = right - triple(split(y_group(k, g)), panel(k), 1)
            store_y(2, g, triple(split(right), panel(2), 1))
            for at in in_group(g):
                for h in range(SUBS):
                    if at == 0:
                        send_y(send, 2, at, h, 0)
                    if at == 1:
                        send_y(send, 2, at, h, 2 + PLANE)
                    if at == 2:
                        send_y(send, 2, at, h, 1)
                    send_y(send, 2, at, h, 3)
        drain(["later"])
        relay(send, 2, True, False)
        for g in range(GROUPS):
            fan_wait(2, g)
            answer = triple(split(y_group(2, g) - fan_group(g)), panel(2), 0)
            send_w[0, rows_of(g)] = triple(split(answer), panel(1), 0)
            send_w_group(send, 0, 0, g, 1)
            if g == 0:
                relay(send, 1, False, False)
            send_w[1, rows_of(g)] = triple(split(answer), panel(0), 0)
            send_w_group(send, 1, 0, g, 0)
            out_ref[:, g * group : (g + 1) * group] = answer.T
        relay(send, 0, False, False)
        send.finish()

    @pl.when(me >= 3)
    def _():
        plane0 = level == 0
        loads["later"].wait()
        later = split(later_ref[...].T)

        def make_term(k):
            load_panel(k)
            term[k] = triple(later, panel(k), 0).reshape(PLANE, SUBS, piece, block)

        def subtract(k):
            value = triple(panel(k), split(y_value(k)), 1)
            out_ref[...] = (t_ref[...] if k == 0 else out_ref[...]) - value

        @pl.when(plane0)
        def _():
            send = Sends()
            for k in range(panels - 1, -1, -1):
                make_term(k)
                for at, device in ((0, 0), (2, 1), (1, 2)):
                    for h in range(SUBS):
                        send(term.at[k, at, h], from_x.at[k, h], x_sem.at[k, h], device)
            loads["t"].wait()

            def take(k):
                for at in range(PLANE):
                    for h in range(SUBS):
                        wait_y(k, at, h)
                        if at == 3:
                            send_y(send, k, at, h, 3 + PLANE)

            take(0)
            take(1)
            relay(send, 2, False, True)
            relay(send, 1, False, True)
            subtract(0)
            subtract(1)
            take(2)
            relay(send, 0, False, True)
            subtract(2)
            send.finish()

        @pl.when(jnp.logical_not(plane0))
        def _():
            far = level == levels - 1
            not_far = jnp.logical_not(far)
            send = Sends()
            for k in range(panels - 1, -1, -1):
                make_term(k)
                for side in range(2):
                    for h in range(SUBS):
                        send(
                            term.at[k, (1 - core) * 2 + side, h], from_core.at[k, side, h],
                            core_sem.at[k, side, h], sibling,
                        )
            for k in range(panels - 1, -1, -1):
                for h in range(SUBS):
                    for side in range(2):
                        arrive(from_core.at[k, side, h], core_sem.at[k, side, h])
                    part_x[k, h] = term[k, facing, h] + from_core[k, 1 - x, h]
                    send(part_x.at[k, h], from_x.at[k, h], x_sem.at[k, h], across)
            loads["t"].wait()

            def line_sum(k, send):
                for h in range(SUBS):
                    arrive(from_x.at[k, h], x_sem.at[k, h])
                    part_z[k, h] = term[k, mine, h] + from_core[k, x, h] + from_x[k, h]

                    @pl.when(not_far)
                    def _():
                        arrive(from_z.at[k, h], z_sem.at[k, h])
                        part_z[k, h] += from_z[k, h]

                    send(part_z.at[k, h], from_z.at[k, h], z_sem.at[k, h], up)

            def take(k, send):
                for h in range(SUBS):
                    wait_y(k, mine, h)
                    send_y(send, k, mine, h, down, not_far)
                    send_y(send, k, mine, h, across)
                    send_y(send, k, mine, h, sibling)

            def pass_on(k, send):
                for h in range(SUBS):
                    wait_y(k, facing, h)
                    send_y(send, k, facing, h, sibling)

            def rest(k):
                for side in range(2):
                    for h in range(SUBS):
                        wait_y(k, (1 - core) * 2 + side, h)

            def middle(order):
                inner_send = Sends()
                inner_send.held = list(send.held)
                done = len(send.held)
                for step, k in order:
                    step(k, inner_send)
                inner_send.held = inner_send.held[done:]
                inner_send.finish()

            steps = {
                "near": [(take, 0), (pass_on, 0), (take, 1), (pass_on, 1), (line_sum, 2), (line_sum, 1), (line_sum, 0)],
                "far": [(line_sum, 2), (line_sum, 1), (line_sum, 0), (take, 0), (pass_on, 0), (take, 1), (pass_on, 1)],
                "mid": [(line_sum, 2), (take, 0), (line_sum, 1), (pass_on, 0), (take, 1), (line_sum, 0), (pass_on, 1)],
            }
            is_near = jnp.logical_and(level == 1, not_far)
            pl.when(is_near)(lambda: middle(steps["near"]))
            pl.when(far)(lambda: middle(steps["far"]))
            pl.when(jnp.logical_and(level > 1, not_far))(lambda: middle(steps["mid"]))
            for k in range(2):
                rest(k)
                subtract(k)
            take(2, send)
            pass_on(2, send)
            rest(2)
            subtract(2)
            send.finish()


def solution(mesh):
    devices = mesh.shape["rows"]

    def local(factor_panels, targets, later_solutions):
        block, rhs = targets.shape
        panels = factor_panels.shape[1] // block
        piece = rhs // PLANE // SUBS
        dma = pltpu.SemaphoreType.DMA
        f32 = jnp.float32
        return pl.pallas_call(
            functools.partial(kernel, devices, panels),
            out_shape=jax.ShapeDtypeStruct((block, rhs), f32),
            in_specs=[pl.BlockSpec(memory_space=pl.ANY)] * 3,
            out_specs=pl.BlockSpec(memory_space=pltpu.VMEM),
            scratch_shapes=[
                pltpu.VMEM((panels, block, block), f32),
                pltpu.VMEM((block, rhs), f32),
                pltpu.VMEM((block, rhs), f32),
                pltpu.VMEM((panels, block, block), jnp.bfloat16),
                pltpu.VMEM((panels, block, block), jnp.bfloat16),
                pltpu.VMEM((panels, PLANE, SUBS, piece, block), f32),
                pltpu.VMEM((panels, PLANE, SUBS, piece, block), f32),
                pltpu.VMEM((panels, 2, SUBS, piece, block), f32),
                pltpu.VMEM((panels, SUBS, piece, block), f32),
                pltpu.VMEM((panels, SUBS, piece, block), f32),
                pltpu.VMEM((panels, SUBS, piece, block), f32),
                pltpu.VMEM((panels, SUBS, piece, block), f32),
                pltpu.VMEM((PLANE, SUBS, piece, block), f32),
                pltpu.VMEM((2, rhs, block), f32),
                pltpu.VMEM((2, rhs, block), f32),
                dma((2 + panels,)),
                dma((128,)),
                dma((panels, PLANE, SUBS)),
                dma((panels, 2, SUBS)),
                dma((panels, SUBS)),
                dma((panels, SUBS)),
                dma((PLANE, SUBS)),
                dma((2, GROUPS)),
            ],
            compiler_params=pltpu.CompilerParams(
                collective_id=0, has_side_effects=True, vmem_limit_bytes=48 * 1024 * 1024
            ),
        )(factor_panels, targets, later_solutions)

    rows = P(("parts", "rows"), None)
    return jax.shard_map(
        local, mesh=mesh, in_specs=(rows, rows, rows), out_specs=rows, check_vma=False
    )
```

time: 504 us -> 60.4 us (0.12)
  waiting for transfers between devices: 455 us -> 0 us
  Pallas kernels: 0 us -> 55.4 us
  matrix products: 31.8 us -> 0 us
  between operations: 13.3 us -> 0.01 us
    psum x5 -> x0, waiting for transfers between devices: 455 us -> none  [the longest x3 275 us: broadcast(): return lax.psum(jnp.where(mine, shard, jnp.zeros_like(shard)), axis)]
    pallas_call x0 -> x1, Pallas kernels: none -> 55.4 us  [local(): pl.pallas_call(functools.partial(kernel, devices, panels), out_shape=jax....]
    dot_general x12 -> x0, matrix products: 31.8 us -> none  [the longest x6 18.3 us: transposed(): lax.dot_general(left, right, (((0,), (0,)), ((), ())), precision=exact_mo...]
  transfers between devices with their start and end apart: 5 -> 0, of which waited for: 5 -> 0; matrix products, arithmetic and copies ran while one was open for 1% -> 0% of each run, Pallas kernels for 0% -> 0%
where the time goes in v1:
time: 60.4 us; the launch traced here: 60.2 us
  Pallas kernels  55.4 us (92%)
  local copies, waits for them, and re-layouts  4.77 us (8%)
    pallas_call x1, Pallas kernels, local(): pl.pallas_call(functools.partial(kernel, devices, panels), out_shape=jax....  55.4 us
    unnamed x7, local copies, waits for them, and re-layouts  4.77 us

profile of v1, /device:TPU:0, one launch (start us, length us, event | category | flops | bytes accessed | tf_op | source)
XLA Modules:
  0.0 60.2 jit_solution(7370505612477973802)
XLA Ops:
  0.0 0.0 copy-start
  0.0 1.9 %copy-done = f32[512,1536]{1,0:T(8,128)S(1)} copy-done((f32[512,1536]{1,0:T(8,128)S(1)}, f32[512,1536]{1,0:T(8,128)}, u32[]{:S(2)}) %copy-start) | copy-done | bytes 3145752
  1.9 0.0 copy-start.1
  1.9 1.0 %copy-done.1 = f32[512,256]{1,0:T(8,128)S(1)} copy-done((f32[512,256]{1,0:T(8,128)S(1)}, f32[512,256]{1,0:T(8,128)}, u32[]{:S(2)}) %copy-start.1) | copy-done | bytes 524312
  2.9 0.0 copy-start.2
  2.9 1.0 %copy-done.2 = f32[512,256]{1,0:T(8,128)S(1)} copy-done((f32[512,256]{1,0:T(8,128)S(1)}, f32[512,256]{1,0:T(8,128)}, u32[]{:S(2)}) %copy-start.2) | copy-done | bytes 524312
  4.0 55.4 %shard_map.37 = f32[512,256]{1,0:T(8,128)S(1)} custom-call(f32[512,1536]{1,0:T(8,128)S(1)} %copy-done, f32[512,256]{1,0:T(8,128)S(1)} %copy-done.1, f32[512,256]{1,0:T(8,128)S(1)} %copy-done.2), custom_call_target="tpu_custom_call" | custom-call | tf_op jit(solution)/shard_map/pallas_call | solution.py:423
  59.4 0.8 %copy.5 = f32[512,256]{1,0:T(8,128)} copy(f32[512,256]{1,0:T(8,128)S(1)} %shard_map.37) | data formatting | bytes 1048576
Async XLA Ops:
  0.0 1.9 %copy-start = (f32[512,1536]{1,0:T(8,128)S(1)}, f32[512,1536]{1,0:T(8,128)}, u32[]{:S(2)}) copy-start(f32[512,1536]{1,0:T(8,128)} %p_hbm.1) | copy-start | bytes 9437188
  1.9 1.0 %copy-start.1 = (f32[512,256]{1,0:T(8,128)S(1)}, f32[512,256]{1,0:T(8,128)}, u32[]{:S(2)}) copy-start(f32[512,256]{1,0:T(8,128)} %t_hbm.1) | copy-start | bytes 1572868
  2.9 1.0 %copy-start.2 = (f32[512,256]{1,0:T(8,128)S(1)}, f32[512,256]{1,0:T(8,128)}, u32[]{:S(2)}) copy-start(f32[512,256]{1,0:T(8,128)} %later_hbm.1) | copy-start | bytes 1572868

commit v2 on v1

v2 whole, which is shorter than its diff:
```python
import functools

import jax
import jax.numpy as jnp
from jax import lax
from jax.experimental import pallas as pl
from jax.experimental.pallas import tpu as pltpu
from jax.sharding import PartitionSpec as P

MESH = pl.DeviceIdType.MESH
PLANE = 4
SUBS = 2
GROUPS = SUBS


def split(value):
    high = value.astype(jnp.bfloat16)
    return high, (value - high.astype(jnp.float32)).astype(jnp.bfloat16)


def triple(left, right, contract):
    def one(a, b):
        return lax.dot_general(
            a, b, (((1,), (contract,)), ((), ())), preferred_element_type=jnp.float32
        )

    return one(left[0], right[0]) + (one(left[0], right[1]) + one(left[1], right[0]))


def kernel(
    devices, panels,
    p_hbm, t_hbm, later_hbm, out_ref,
    p_ref, t_ref, later_ref, p_high, p_low,
    y_ref, term, from_core, from_x, from_z, part_x, part_z, fan, send_w, got_w,
    in_sem, send_sem, y_sem, core_sem, x_sem, z_sem, fan_sem, w_sem,
):
    block, rhs = t_ref.shape
    levels = devices // PLANE
    piece = rhs // PLANE // SUBS
    group = rhs // GROUPS
    me = lax.axis_index("rows")
    level, q = me // PLANE, me % PLANE
    x, core = q // 2, q % 2
    mine = core * 2 + x
    facing = core * 2 + 1 - x
    sibling = me + 1 - 2 * core
    across = me + 2 - 4 * x
    up, down = me - PLANE, me + PLANE

    loads = {"t": pltpu.make_async_copy(t_hbm, t_ref, in_sem.at[0])}
    loads["later"] = pltpu.make_async_copy(later_hbm, later_ref, in_sem.at[1])
    for k in range(panels):
        loads[k] = pltpu.make_async_copy(
            p_hbm.at[:, k * block : (k + 1) * block], p_ref.at[k], in_sem.at[2 + k]
        )
    for name in ["t", 0, "later"] + list(range(panels - 1, 0, -1)):
        loads[name].start()

    barrier = pltpu.get_barrier_semaphore()
    for step in range(1, PLANE):
        other = level * PLANE + (q + step) % PLANE
        pl.semaphore_signal(barrier, inc=1, device_id={"rows": other}, device_id_type=MESH)

    @pl.when(level > 0)
    def _():
        pl.semaphore_signal(barrier, inc=1, device_id={"rows": up}, device_id_type=MESH)

    @pl.when(level < levels - 1)
    def _():
        pl.semaphore_signal(barrier, inc=1, device_id={"rows": down}, device_id_type=MESH)

    inner = jnp.logical_and(level > 0, level < levels - 1)

    def enter():
        @pl.when(inner)
        def _():
            pl.semaphore_wait(barrier, PLANE + 1)

        @pl.when(jnp.logical_not(inner))
        def _():
            pl.semaphore_wait(barrier, PLANE)

    class Sends:
        def __init__(self, me=None):
            self.held = []
            self.me = me

        def __call__(self, src, dst, recv, device, when=None):
            copy = pltpu.make_async_remote_copy(
                src_ref=src, dst_ref=dst, send_sem=send_sem.at[len(self.held)], recv_sem=recv,
                device_id={"rows": device}, device_id_type=MESH,
            )
            self.held.append((copy, when))
            if when is None:
                copy.start()
            else:
                pl.when(when)(copy.start)

        def finish(self):
            for copy, when in self.held:
                if when is None:
                    copy.wait_send()
                else:
                    pl.when(when)(copy.wait_send)

    def arrive(ref, sem):
        pltpu.make_async_remote_copy(
            src_ref=ref, dst_ref=ref, send_sem=send_sem.at[0], recv_sem=sem,
            device_id={"rows": sibling}, device_id_type=MESH,
        ).wait_recv()

    def send_y(send, k, at, h, device, when=None):
        send(y_ref.at[k, h, at], y_ref.at[k, h, at], y_sem.at[k, h, at], device, when)

    def wait_y(k, at, h):
        arrive(y_ref.at[k, h, at], y_sem.at[k, h, at])

    def y_value(k):
        return y_ref[k].reshape(rhs, block)

    def y_group(k, g):
        return y_ref[k, g].reshape(group, block)

    def fan_group(g):
        return fan[g].reshape(group, block)

    def store_y(k, g, value):
        y_ref[k, g] = value.reshape(PLANE, piece, block)

    def load_panel(k):
        loads[k].wait()
        high, low = split(p_ref[k])
        p_high[k] = high
        p_low[k] = low

    def panel(k):
        return p_high[k], p_low[k]

    def rows_of(g):
        return pl.ds(g * group, group)

    def relay(send, k, h):
        for side in range(2):
            at = core * 2 + side
            arrive(from_z.at[k, h, side], z_sem.at[k, h, side])
            value = from_z[k, h, side]
            if send.me == 3:
                value = value + term[k, h, at]
            else:
                arrive(from_x.at[k, h, side], x_sem.at[k, h, side])
                value = value + from_x[k, h, side]
            if send.me == k:
                fan[h, at] = value
            else:
                part_z[k, h, side] = value
                send(part_z.at[k, h, side], fan.at[h, at], fan_sem.at[h, at], k)

    def fan_wait(owner, h):
        other = 1 - owner % 2
        for at in (other * 2, other * 2 + 1):
            arrive(fan.at[h, at], fan_sem.at[h, at])

    def send_w_group(send, slot, to_slot, g, device):
        send(send_w.at[slot, rows_of(g)], got_w.at[to_slot, rows_of(g)], w_sem.at[to_slot, g], device)

    def wait_w(slot, g):
        arrive(got_w.at[slot, rows_of(g)], w_sem.at[slot, g])

    def drain(names):
        for name in names:
            loads[name].wait()

    @pl.when(me == 0)
    def _():
        send = Sends(0)
        loads["t"].wait()
        load_panel(0)
        target = t_ref[...].T
        for g in range(GROUPS):
            store_y(0, g, triple(split(target[g * group : (g + 1) * group]), panel(0), 1))
            if g == 0:
                enter()
            for at in range(PLANE):
                send_y(send, 0, at, g, 1)
                send_y(send, 0, at, g, 2)
                if at == 0:
                    send_y(send, 0, at, g, PLANE)
        drain(["later", 1, 2])
        for h in range(SUBS):
            wait_y(1, 0, h)
            send_y(send, 1, 0, h, PLANE)
        for h in range(SUBS):
            relay(send, 1, h)
        for h in range(SUBS):
            wait_y(2, 0, h)
            send_y(send, 2, 0, h, PLANE)
        for h in range(SUBS):
            relay(send, 0, h)
        for g in range(GROUPS):
            fan_wait(0, g)
            wait_w(0, g)
            right = y_group(0, g) - fan_group(g) - got_w[0, rows_of(g)]
            wait_w(1, g)
            answer = triple(split(right - got_w[1, rows_of(g)]), panel(0), 0)
            out_ref[:, g * group : (g + 1) * group] = answer.T
        send.finish()

    @pl.when(me == 1)
    def _():
        send = Sends(1)
        loads["t"].wait()
        target = t_ref[...].T
        load_panel(0)
        load_panel(1)
        enter()
        for g in range(GROUPS):
            for at in range(PLANE):
                wait_y(0, at, g)
                if at == 2:
                    send_y(send, 0, at, g, 1 + PLANE)
            right = target[g * group : (g + 1) * group] - triple(split(y_group(0, g)), panel(0), 1)
            store_y(1, g, triple(split(right), panel(1), 1))
            for at in range(PLANE):
                send_y(send, 1, at, g, 2)
                if at == 2:
                    send_y(send, 1, at, g, 1 + PLANE)
                if at == 0:
                    send_y(send, 1, at, g, 0)
        drain(["later", 2])
        for h in range(SUBS):
            relay(send, 1, h)
        for h in range(SUBS):
            wait_y(2, 2, h)
            send_y(send, 2, 2, h, 1 + PLANE)
        for h in range(SUBS):
            relay(send, 0, h)
        for g in range(GROUPS):
            fan_wait(1, g)
            right = y_group(1, g) - fan_group(g)
            wait_w(0, g)
            answer = triple(split(right - got_w[0, rows_of(g)]), panel(1), 0)
            send_w[0, rows_of(g)] = triple(split(answer), panel(0), 0)
            send_w_group(send, 0, 1, g, 0)
            out_ref[:, g * group : (g + 1) * group] = answer.T
        send.finish()

    @pl.when(me == 2)
    def _():
        send = Sends(2)
        loads["t"].wait()
        target = t_ref[...].T
        for k in range(panels):
            load_panel(k)
        enter()
        for g in range(GROUPS):
            right = target[g * group : (g + 1) * group]
            for k in range(2):
                for at in range(PLANE):
                    wait_y(k, at, g)
                    send_y(send, k, at, g, 3)
                    if at == 1:
                        send_y(send, k, at, g, 2 + PLANE)
                right = right - triple(split(y_group(k, g)), panel(k), 1)
            store_y(2, g, triple(split(right), panel(2), 1))
            for at in range(PLANE):
                if at == 0:
                    send_y(send, 2, at, g, 0)
                if at == 1:
                    send_y(send, 2, at, g, 2 + PLANE)
                if at == 2:
                    send_y(send, 2, at, g, 1)
                send_y(send, 2, at, g, 3)
        drain(["later"])
        for g in range(GROUPS):
            relay(send, 2, g)
            fan_wait(2, g)
            answer = triple(split(y_group(2, g) - fan_group(g)), panel(2), 0)
            send_w[0, rows_of(g)] = triple(split(answer), panel(1), 0)
            send_w_group(send, 0, 0, g, 1)
            send_w[1, rows_of(g)] = triple(split(answer), panel(0), 0)
            send_w_group(send, 1, 0, g, 0)
            out_ref[:, g * group : (g + 1) * group] = answer.T
        send.finish()

    @pl.when(me >= 3)
    def _():
        plane0 = level == 0
        loads["later"].wait()
        later = split(later_ref[...].T)

        def make_term(k):
            load_panel(k)
            term[k] = triple(later, panel(k), 0).reshape(SUBS, PLANE, piece, block)

        def subtract(k):
            value = triple(panel(k), split(y_value(k)), 1)
            out_ref[...] = (t_ref[...] if k == 0 else out_ref[...]) - value

        make_term(panels - 1)
        enter()

        @pl.when(plane0)
        def _():
            send = Sends(3)
            for k in range(panels - 1, -1, -1):
                if k < panels - 1:
                    make_term(k)
                for h in range(SUBS):
                    for at in range(PLANE):
                        device = k // 2 * 2 + at // 2
                        if device != 3:
                            send(
                                term.at[k, h, at], from_x.at[k, h, at % 2],
                                x_sem.at[k, h, at % 2], device,
                            )
            loads["t"].wait()

            def take(k):
                for h in range(SUBS):
                    for at in range(PLANE):
                        wait_y(k, at, h)
                        if at == 3:
                            send_y(send, k, at, h, 3 + PLANE)

            take(0)
            take(1)
            subtract(0)
            take(2)
            for h in range(SUBS):
                relay(send, 2, h)
            subtract(1)
            subtract(2)
            send.finish()

        @pl.when(jnp.logical_not(plane0))
        def _():
            far = level == levels - 1
            not_far = jnp.logical_not(far)
            send = Sends()
            for k in range(panels - 1, -1, -1):
                if k < panels - 1:
                    make_term(k)
                for h in range(SUBS):
                    for side in range(2):
                        send(
                            term.at[k, h, (1 - core) * 2 + side], from_core.at[k, h, side],
                            core_sem.at[k, h, side], sibling,
                        )
            loads["t"].wait()
            for k in range(panels - 1, -1, -1):
                for h in range(SUBS):
                    for side in range(2):
                        arrive(from_core.at[k, h, side], core_sem.at[k, h, side])
                        part_x[k, h, side] = term[k, h, core * 2 + side] + from_core[k, h, side]
                        send(
                            part_x.at[k, h, side], from_x.at[k, h, side],
                            x_sem.at[k, h, side], across, x != k // 2,
                        )

            def line_sum(k, send):
                here = x == k // 2
                for h in range(SUBS):
                    for side in range(2):

                        @pl.when(here)
                        def _():
                            arrive(from_x.at[k, h, side], x_sem.at[k, h, side])
                            part_z[k, h, side] = part_x[k, h, side] + from_x[k, h, side]

                        @pl.when(jnp.logical_and(here, not_far))
                        def _():
                            arrive(from_z.at[k, h, side], z_sem.at[k, h, side])
                            part_z[k, h, side] += from_z[k, h, side]

                        send(
                            part_z.at[k, h, side], from_z.at[k, h, side],
                            z_sem.at[k, h, side], up, here,
                        )

            def take(k, send):
                for h in range(SUBS):
                    wait_y(k, mine, h)
                    send_y(send, k, mine, h, down, not_far)
                    send_y(send, k, mine, h, across)
                    send_y(send, k, mine, h, sibling)

            def pass_on(k, send):
                for h in range(SUBS):
                    wait_y(k, facing, h)
                    send_y(send, k, facing, h, sibling)

            def rest(k):
                for h in range(SUBS):
                    for side in range(2):
                        wait_y(k, (1 - core) * 2 + side, h)

            def middle(order):
                inner_send = Sends()
                inner_send.held = list(send.held)
                done = len(send.held)
                for step, k in order:
                    step(k, inner_send)
                inner_send.held = inner_send.held[done:]
                inner_send.finish()

            last = [(pass_on, 0), (pass_on, 1)]
            steps = {
                "near": [(take, 0), (line_sum, 2), (take, 1), (line_sum, 1), (line_sum, 0)] + last,
                "far": [(line_sum, 2), (line_sum, 1), (line_sum, 0), (take, 0), (take, 1)] + last,
                "mid": [(line_sum, 2), (take, 0), (line_sum, 1), (take, 1), (line_sum, 0)] + last,
            }
            is_near = jnp.logical_and(level == 1, not_far)
            pl.when(is_near)(lambda: middle(steps["near"]))
            pl.when(far)(lambda: middle(steps["far"]))
            pl.when(jnp.logical_and(level > 1, not_far))(lambda: middle(steps["mid"]))
            for k in range(2):
                rest(k)
                subtract(k)
            take(2, send)
            pass_on(2, send)
            rest(2)
            subtract(2)
            send.finish()


def solution(mesh):
    devices = mesh.shape["rows"]

    def local(factor_panels, targets, later_solutions):
        block, rhs = targets.shape
        panels = factor_panels.shape[1] // block
        piece = rhs // PLANE // SUBS
        dma = pltpu.SemaphoreType.DMA
        f32 = jnp.float32
        return pl.pallas_call(
            functools.partial(kernel, devices, panels),
            out_shape=jax.ShapeDtypeStruct((block, rhs), f32),
            in_specs=[pl.BlockSpec(memory_space=pltpu.HBM)] * 3,
            out_specs=pl.BlockSpec(memory_space=pltpu.VMEM),
            scratch_shapes=[
                pltpu.VMEM((panels, block, block), f32),
                pltpu.VMEM((block, rhs), f32),
                pltpu.VMEM((block, rhs), f32),
                pltpu.VMEM((panels, block, block), jnp.bfloat16),
                pltpu.VMEM((panels, block, block), jnp.bfloat16),
                pltpu.VMEM((panels, SUBS, PLANE, piece, block), f32),
                pltpu.VMEM((panels, SUBS, PLANE, piece, block), f32),
                pltpu.VMEM((panels, SUBS, 2, piece, block), f32),
                pltpu.VMEM((panels, SUBS, 2, piece, block), f32),
                pltpu.VMEM((panels, SUBS, 2, piece, block), f32),
                pltpu.VMEM((panels, SUBS, 2, piece, block), f32),
                pltpu.VMEM((panels, SUBS, 2, piece, block), f32),
                pltpu.VMEM((SUBS, PLANE, piece, block), f32),
                pltpu.VMEM((2, rhs, block), f32),
                pltpu.VMEM((2, rhs, block), f32),
                dma((2 + panels,)),
                dma((256,)),
                dma((panels, SUBS, PLANE)),
                dma((panels, SUBS, 2)),
                dma((panels, SUBS, 2)),
                dma((panels, SUBS, 2)),
                dma((SUBS, PLANE)),
                dma((2, GROUPS)),
            ],
            compiler_params=pltpu.CompilerParams(
                collective_id=0, has_side_effects=True, vmem_limit_bytes=62 * 1024 * 1024
            ),
        )(factor_panels, targets, later_solutions)

    rows = P(("parts", "rows"), None)
    return jax.shard_map(
        local, mesh=mesh, in_specs=(rows, rows, rows), out_specs=rows, check_vma=False
    )
```

time: 60.4 us -> 47.1 us (0.78); the launches traced: 60.2 us -> 46.2 us
  Pallas kernels: 55.4 us -> 44.4 us
  local copies, waits for them, and re-layouts: 4.77 us -> 1.87 us
    pallas_call x1, Pallas kernels: 55.4 us -> 44.4 us  [local(): pl.pallas_call(functools.partial(kernel, devices, panels), out_shape=jax....]
    unnamed x7 -> x1, local copies, waits for them, and re-layouts: 4.77 us -> 1.87 us
where the time goes in v2:
time: 47.1 us; the launch traced here: 46.2 us
  Pallas kernels  44.4 us (94%)
  local copies, waits for them, and re-layouts  1.87 us (4%)
    pallas_call x1, Pallas kernels, local(): pl.pallas_call(functools.partial(kernel, devices, panels), out_shape=jax....  44.4 us
    unnamed x1, local copies, waits for them, and re-layouts  1.87 us

profile of v2, /device:TPU:0, one launch (start us, length us, event | category | flops | bytes accessed | tf_op | source)
XLA Modules:
  0.0 46.2 jit_solution(12189007282660988540)
XLA Ops:
  0.0 44.4 %shard_map.37 = f32[512,256]{1,0:T(8,128)} custom-call(f32[512,1536]{1,0:T(8,128)} %p_hbm.1, f32[512,256]{1,0:T(8,128)} %t_hbm.1, f32[512,256]{1,0:T(8,128)} %later_hbm.1), custom_call_target="tpu_custom_call" | custom-call | tf_op jit(solution)/shard_map/pallas_call | solution.py:435
  44.4 1.9 %copy.5 = f32[512,256]{1,0:T(8,128)} copy(f32[512,256]{1,0:T(8,128)} %shard_map.37) | data formatting | bytes 1048576

commit v3 on v2

--- a/solution.py
+++ b/solution.py
@@ -9,8 +9,9 @@
 
 MESH = pl.DeviceIdType.MESH
 PLANE = 4
-SUBS = 2
+SUBS = 4
 GROUPS = SUBS
+SHARED = 2
 
 
 def split(value):
@@ -140,8 +141,8 @@
         return pl.ds(g * group, group)
 
     def relay(send, k, h):
-        for side in range(2):
-            at = core * 2 + side
+        for side in range(1 if k == SHARED else 2):
+            at = mine if k == SHARED else core * 2 + side
             arrive(from_z.at[k, h, side], z_sem.at[k, h, side])
             value = from_z[k, h, side]
             if send.me == 3:
@@ -156,8 +157,11 @@
                 send(part_z.at[k, h, side], fan.at[h, at], fan_sem.at[h, at], k)
 
     def fan_wait(owner, h):
-        other = 1 - owner % 2
-        for at in (other * 2, other * 2 + 1):
+        if owner == SHARED:
+            others = [at for at in range(PLANE) if at != owner % 2 * 2 + owner // 2]
+        else:
+            others = [(1 - owner % 2) * 2, (1 - owner % 2) * 2 + 1]
+        for at in others:
             arrive(fan.at[h, at], fan_sem.at[h, at])
 
     def send_w_group(send, slot, to_slot, g, device):
@@ -189,8 +193,9 @@
         for h in range(SUBS):
             wait_y(1, 0, h)
             send_y(send, 1, 0, h, PLANE)
-        for h in range(SUBS):
-            relay(send, 1, h)
+        for k in (2, 1):
+            for h in range(SUBS):
+                relay(send, k, h)
         for h in range(SUBS):
             wait_y(2, 0, h)
             send_y(send, 2, 0, h, PLANE)
@@ -227,8 +232,9 @@
                 if at == 0:
                     send_y(send, 1, at, g, 0)
         drain(["later", 2])
-        for h in range(SUBS):
-            relay(send, 1, h)
+        for k in (2, 1):
+            for h in range(SUBS):
+                relay(send, k, h)
         for h in range(SUBS):
             wait_y(2, 2, h)
             send_y(send, 2, 2, h, 1 + PLANE)
@@ -277,6 +283,9 @@
             answer = triple(split(y_group(2, g) - fan_group(g)), panel(2), 0)
             send_w[0, rows_of(g)] = triple(split(answer), panel(1), 0)
             send_w_group(send, 0, 0, g, 1)
+            got_w[0, rows_of(g)] = answer
+        for g in range(GROUPS):
+            answer = got_w[0, rows_of(g)]
             send_w[1, rows_of(g)] = triple(split(answer), panel(0), 0)
             send_w_group(send, 1, 0, g, 0)
             out_ref[:, g * group : (g + 1) * group] = answer.T
@@ -307,11 +316,13 @@
                     make_term(k)
                 for h in range(SUBS):
                     for at in range(PLANE):
-                        device = k // 2 * 2 + at // 2
+                        device, slot = k // 2 * 2 + at // 2, at % 2
+                        if k == SHARED:
+                            device, slot = at % 2 * 2 + at // 2, 0
                         if device != 3:
                             send(
-                                term.at[k, h, at], from_x.at[k, h, at % 2],
-                                x_sem.at[k, h, at % 2], device,
+                                term.at[k, h, at], from_x.at[k, h, slot],
+                                x_sem.at[k, h, slot], device,
                             )
             loads["t"].wait()
 
@@ -351,6 +362,12 @@
                 for h in range(SUBS):
                     for side in range(2):
                         arrive(from_core.at[k, h, side], core_sem.at[k, h, side])
+                    if k == SHARED:
+                        part_x[k, h, 1] = term[k, h, facing] + from_core[k, h, 1 - x]
+                        send(part_x.at[k, h, 1], from_x.at[k, h, 0], x_sem.at[k, h, 0], across)
+                        part_x[k, h, 0] = term[k, h, mine] + from_core[k, h, x]
+                        continue
+                    for side in range(2):
                         part_x[k, h, side] = term[k, h, core * 2 + side] + from_core[k, h, side]
                         send(
                             part_x.at[k, h, side], from_x.at[k, h, side],
@@ -358,9 +375,9 @@
                         )
 
             def line_sum(k, send):
-                here = x == k // 2
-                for h in range(SUBS):
-                    for side in range(2):
+                here = always if k == SHARED else at_x[k // 2]
+                for h in range(SUBS):
+                    for side in range(1 if k == SHARED else 2):
 
                         @pl.when(here)
                         def _():
@@ -393,6 +410,22 @@
                 for h in range(SUBS):
                     for side in range(2):
                         wait_y(k, (1 - core) * 2 + side, h)
+
+            middles = []
+            at_x = [x == 0, x == 1]
+            always = level > 0
+
+            def sent(first, conditions):
+                for index, when in enumerate(conditions):
+                    wait = pltpu.make_async_remote_copy(
+                        src_ref=part_z.at[0, 0, 0], dst_ref=part_z.at[0, 0, 0],
+                        send_sem=send_sem.at[first + index], recv_sem=z_sem.at[0, 0, 0],
+                        device_id={"rows": sibling}, device_id_type=MESH,
+                    ).wait_send
+                    if when is None:
+                        wait()
+                    else:
+                        pl.when(when)(wait)
 
             def middle(order):
                 inner_send = Sends()
@@ -400,27 +433,32 @@
                 done = len(send.held)
                 for step, k in order:
                     step(k, inner_send)
-                inner_send.held = inner_send.held[done:]
-                inner_send.finish()
-
-            last = [(pass_on, 0), (pass_on, 1)]
+                middles.append([when for _, when in inner_send.held[done:]])
+
             steps = {
-                "near": [(take, 0), (line_sum, 2), (take, 1), (line_sum, 1), (line_sum, 0)] + last,
-                "far": [(line_sum, 2), (line_sum, 1), (line_sum, 0), (take, 0), (take, 1)] + last,
-                "mid": [(line_sum, 2), (take, 0), (line_sum, 1), (take, 1), (line_sum, 0)] + last,
+                "near": [(take, 0), (line_sum, 2), (take, 1), (line_sum, 1), (pass_on, 0), (take, 2), (line_sum, 0)],
+                "far": [(line_sum, 2), (line_sum, 1), (line_sum, 0), (take, 0), (take, 1), (pass_on, 0), (take, 2)],
+                "mid": [(line_sum, 2), (take, 0), (line_sum, 1), (take, 1), (line_sum, 0), (pass_on, 0), (take, 2)],
             }
             is_near = jnp.logical_and(level == 1, not_far)
+            is_mid = jnp.logical_and(level > 1, not_far)
             pl.when(is_near)(lambda: middle(steps["near"]))
             pl.when(far)(lambda: middle(steps["far"]))
-            pl.when(jnp.logical_and(level > 1, not_far))(lambda: middle(steps["mid"]))
-            for k in range(2):
-                rest(k)
-                subtract(k)
-            take(2, send)
+            pl.when(is_mid)(lambda: middle(steps["mid"]))
+            first = len(send.held)
+            send.held += [None] * len(middles[0])
+            pass_on(1, send)
+            rest(0)
+            subtract(0)
+            rest(1)
             pass_on(2, send)
+            subtract(1)
             rest(2)
             subtract(2)
+            send.held = send.held[:first] + send.held[first + len(middles[0]) :]
             send.finish()
+            for branch, conditions in zip((is_near, far, is_mid), middles):
+                pl.when(branch)(functools.partial(sent, first, conditions))
 
 
 def solution(mesh):

time: 47.1 us -> 46.2 us (0.981); the launches traced: 46.2 us -> 46 us
  no operation moved by 1% of the time
where the time goes in v3:
time: 46.2 us; the launch traced here: 46 us
  Pallas kernels  44.2 us (96%)
  local copies, waits for them, and re-layouts  1.87 us (4%)
    pallas_call x1, Pallas kernels, local(): pl.pallas_call(functools.partial(kernel, devices, panels), out_shape=jax....  44.2 us
    unnamed x1, local copies, waits for them, and re-layouts  1.87 us

profile of v3, /device:TPU:0, one launch (start us, length us, event | category | flops | bytes accessed | tf_op | source)
XLA Modules:
  0.0 46.0 jit_solution(5567376461685827993)
XLA Ops:
  0.0 44.2 %shard_map.37 = f32[512,256]{1,0:T(8,128)} custom-call(f32[512,1536]{1,0:T(8,128)} %p_hbm.1, f32[512,256]{1,0:T(8,128)} %t_hbm.1, f32[512,256]{1,0:T(8,128)} %later_hbm.1), custom_call_target="tpu_custom_call" | custom-call | tf_op jit(solution)/shard_map/pallas_call | solution.py:473
  44.2 1.9 %copy.5 = f32[512,256]{1,0:T(8,128)} copy(f32[512,256]{1,0:T(8,128)} %shard_map.37) | data formatting | bytes 1048576
